TPU v7x, 512 devices: a whole 4x4x16 slice. The times are simulated.
512 devices in a mesh: blk: 32 (over z, x_hi), uly: 16 (over y, x_lo, core).
Axes of the slice: x: 4 (x_hi: 2, x_lo: 2; x = x_hi * 2 + x_lo), y: 4, z: 16, core: 2. Of those that a mesh axis runs over, the one named last changes fastest.
Arguments:
- queries: bfloat16 [16384, 2048], P(('blk', 'uly')), may hold values from -140 to 140
- keys: bfloat16 [16384, 2048], P(('blk', 'uly')), may hold values from -5 to 5
- values: bfloat16 [16384, 2048], P(('blk', 'uly')), may hold values from -6 to 6
- tile_mask: int32 [32, 32, 4, 4], replicated, may hold values from 0 to 1, as said below
- frame_order: int32 [32], replicated, may hold values from 0 to 31, each once
Outputs:
- attended: bfloat16 [16384, 2048], P(('blk', 'uly'))
Inputs may be any that keep to these rules, and one draw needn't show every extreme that they name: `tile_mask`: every tile attends the same tile of its own frame. For two different frames, exactly 2 key tiles of the key frame are attended by some query tile of the query frame. `frame_order`: each frame number appears once.
All inputs are finite; a program needn't handle non-finite values.
Results may differ from a plain program's by a relative error of at most 0.009.
Values may be sent and summed in bfloat16 or wider, within the bound.
A program may use at most 64 MiB of HBM per device.

v0:
```python
import math

import jax
import jax.numpy as jnp
from jax import lax
from jax.sharding import PartitionSpec as P

HD = 128
TILE = 128


def per_device(queries, keys, values, tile_mask, frame_order):
    query_heads, key_heads, value_heads = (
        lax.all_to_all(queries, "uly", split_axis=1, concat_axis=0, tiled=True),
        lax.all_to_all(keys, "uly", split_axis=1, concat_axis=0, tiled=True),
        lax.all_to_all(values, "uly", split_axis=1, concat_axis=0, tiled=True),
    )
    row_count = query_heads.shape[0]
    head_count = query_heads.shape[1] // HD
    query_tiles = row_count // TILE
    query_three = query_heads.reshape(row_count, head_count, HD)
    kv_pair = jnp.stack([key_heads, value_heads])
    cycle_index = lax.axis_index("blk")
    own_frame = frame_order[cycle_index]
    frame_rows = lax.dynamic_index_in_dim(tile_mask, own_frame, 0, keepdims=False)
    score_scale = 1.0 / math.sqrt(HD)

    def block_update(carried, kv_block, key_tile_ids, tile_valid):
        block_width = kv_block.shape[1]
        key_tiles = block_width // TILE
        key_frames = jnp.take(frame_order, key_tile_ids // query_tiles)
        chosen = frame_rows[key_frames, :, key_tile_ids % query_tiles]
        allowed = (jnp.transpose(chosen) > 0) & tile_valid[None, :]
        mask_five = allowed[None, :, None, :, None]
        running_max, running_sum, weighted = carried
        key_three = kv_block[0].reshape(block_width, head_count, HD)
        value_three = kv_block[1].reshape(block_width, head_count, HD)
        scores = (
            jnp.einsum("qhd,khd->hqk", query_three, key_three, preferred_element_type=jnp.float32)
            * score_scale
        )
        scores = scores.reshape(head_count, query_tiles, TILE, key_tiles, TILE)
        block_max = jnp.max(jnp.where(mask_five, scores, -1e30), axis=(3, 4)).reshape(
            head_count, row_count
        )
        new_max = jnp.maximum(running_max, block_max)
        factor = jnp.exp(running_max - new_max)
        shifted = new_max.reshape(head_count, query_tiles, TILE, 1, 1)
        probs = jnp.where(mask_five, jnp.exp(scores - shifted), 0.0).reshape(
            head_count, row_count, block_width
        )
        new_sum = running_sum * factor + jnp.sum(probs, axis=-1)
        mixed = jnp.einsum(
            "hqk,khd->qhd",
            probs.astype(jnp.bfloat16),
            value_three,
            preferred_element_type=jnp.float32,
        )
        new_weighted = weighted * jnp.transpose(factor)[:, :, None] + mixed
        return (new_max, new_sum, new_weighted)

    initial = (
        jnp.full((head_count, row_count), -1e30, jnp.float32),
        jnp.zeros((head_count, row_count), jnp.float32),
        jnp.zeros((row_count, head_count, HD), jnp.float32),
    )
    carried = initial
    kv_piece = lax.all_gather(kv_pair, "blk", axis=1, tiled=True)
    piece_width = kv_piece.shape[1]
    block_width = 4 * row_count
    blocks = piece_width // block_width
    block_tiles = block_width // TILE

    def block_step(kept, number):
        block_part = lax.dynamic_slice_in_dim(kv_piece, number * block_width, block_width, 1)
        tile_ids = number * block_width // TILE + jnp.arange(block_tiles, dtype=jnp.int32)
        return (block_update(kept, block_part, tile_ids, jnp.ones((block_tiles,), bool)), None)

    carried, _ = lax.scan(block_step, carried, jnp.arange(blocks, dtype=jnp.int32))
    running_max, running_sum, weighted = carried
    output = (weighted / jnp.transpose(running_sum)[:, :, None]).astype(jnp.bfloat16)
    output = output.reshape(row_count, head_count * HD)
    return lax.all_to_all(output, "uly", split_axis=0, concat_axis=1, tiled=True)


def solution(mesh):
    return jax.shard_map(
        per_device,
        mesh=mesh,
        in_specs=(
            P(("blk", "uly"), None),
            P(("blk", "uly"), None),
            P(("blk", "uly"), None),
            P(),
            P(),
        ),
        out_specs=P(("blk", "uly"), None),
        check_vma=False,
    )
```

profile of v0, /device:TPU:1, one launch (start us, length us, event | category | flops | bytes accessed | tf_op | source)
XLA Modules:
  0.0 321.6 jit_solution(2918287343510439599)
XLA Ops:
  6.5 1.6 copy_bitcast_fusion.3
  8.2 10.2 %all-to-all-start = ((bf16[32,16,128]{2,0,1:T(8,128)(2,1)}), bf16[32,16,128]{2,0,1:T(8,128)(2,1)S(1)}, u32[]{:S(2)}, u32[]{:S(2)}) async-start(bf16[32,16,128]{2,0,1:T(8,128)(2,1)} %copy_bitcast_fusion.3), calls=%async_computation | async-start | bytes 262144 | tf_op jit(solution)/shard_map/all_to_all | solution.py:15
  19.3 5.2 %all-to-all-done = bf16[32,16,128]{2,0,1:T(8,128)(2,1)S(1)} async-done(((bf16[32,16,128]{2,0,1:T(8,128)(2,1)}), bf16[32,16,128]{2,0,1:T(8,128)(2,1)S(1)}, u32[]{:S(2)}, u32[]{:S(2)}) %all-to-all-start) | async-done | bytes 131104 | tf_op jit(solution)/shard_map/all_to_all | solution.py:15
  24.6 9.3 %all_to_all.67 = bf16[32,16,128]{2,0,1:T(8,128)(2,1)S(1)} all-to-all(bf16[32,16,128]{2,0,1:T(8,128)(2,1)S(1)} %copy_bitcast_fusion.2), channel_id=1, replica_groups=mesh['blk'=32,'uly'=16] {'uly'}, dimensions={1} | all-to-all | bytes 262144 | tf_op jit(solution)/shard_map/all_to_all | solution.py:16
  34.6 1.6 copy_bitcast_fusion.1
  36.2 4.0 %all-to-all-start.2 = ((bf16[32,16,128]{2,0,1:T(8,128)(2,1)}), bf16[32,16,128]{2,0,1:T(8,128)(2,1)S(1)}, u32[]{:S(2)}, u32[]{:S(2)}) async-start(bf16[32,16,128]{2,0,1:T(8,128)(2,1)} %copy_bitcast_fusion.1), calls=%async_computation.2 | async-start | bytes 262144 | tf_op jit(solution)/shard_map/all_to_all | solution.py:14
  43.3 3.1 all-to-all-done.2
  46.4 172.4 %all-gather.2.cloned.1.call-done = bf16[2,16384,128]{2,1,0:T(8,128)(2,1)} async-done(((bf16[2,512,128]{2,1,0:T(8,128)(2,1)}), bf16[2,16384,128]{2,1,0:T(8,128)(2,1)}) %all-gather.2.cloned.1.call-update) | async-done | bytes 8388624 | tf_op jit(solution)/shard_map/all_gather | solution.py:68
  218.9 76.3 %while.18 = (s32[]{:T(128)}, f32[1,512]{1,0:T(1,128)S(1)}, f32[1,512]{1,0:T(1,128)S(1)}, f32[512,1,128]{0,2,1:T(8,128)S(1)}, s32[8]{0:T(128)S(1)}, /*index=5*/s3...) while((s32[]{:T(128)}, f32[1,512]{1,0:T(1,128)S(1)}, ...), condition=%wide.region_3.4_spmd.clone, body=%wide.region_0.3_spmd.clone.sunk | while | flops 548606464 | bytes 18519896 | solution.py:79
  220.2 1.3 gather_fusion
  222.8 2.0 fusion.44
  226.0 2.4 fusion.48
  229.7 1.3 gather_fusion
  232.3 2.0 fusion.44
  235.5 2.4 fusion.48
  239.3 1.3 gather_fusion
  241.8 2.0 fusion.44
  245.1 2.4 fusion.48
  251.4 2.0 fusion.44
  254.6 2.4 fusion.48
  258.3 1.3 gather_fusion
  260.9 2.0 fusion.44
  264.2 2.4 fusion.48
  267.9 1.3 gather_fusion
  270.5 2.0 fusion.44
  273.7 2.4 fusion.48
  280.0 2.0 fusion.44
  283.3 2.4 fusion.48
  287.0 1.3 gather_fusion
  289.5 2.0 fusion.44
  292.8 2.4 fusion.48
  295.5 18.6 %all_to_all.68 = bf16[16,32,128]{2,1,0:T(8,128)(2,1)S(1)} all-to-all(bf16[16,32,128]{2,1,0:T(8,128)(2,1)S(1)} %bitcast.150), channel_id=1, replica_groups=mesh['blk'=32,'uly'=16] {'uly'}, dimensions={0} | all-to-all | bytes 262144 | tf_op jit(solution)/shard_map/all_to_all | solution.py:83
  (106 shorter events, 31.1 us)
Async XLA Ops:
  6.5 36.6 %copy-start = (s32[32,32,4,4]{1,3,2,0:T(4,128)S(1)}, s32[32,32,4,4]{1,3,2,0:T(4,128)}, u32[]{:S(2)}) copy-start(s32[32,32,4,4]{1,3,2,0:T(4,128)} %param.10) | copy-start | bytes 196612
  8.2 16.4 %all-to-all-start = ((bf16[32,16,128]{2,0,1:T(8,128)(2,1)}), bf16[32,16,128]{2,0,1:T(8,128)(2,1)S(1)}, u32[]{:S(2)}, u32[]{:S(2)}) async-start(bf16[32,16,128]{2,0,1:T(8,128)(2,1)} %copy_bitcast_fusion.3), calls=%async_computation | async-start | bytes 262144 | tf_op jit(solution)/shard_map/all_to_all | solution.py:15
  18.3 200.5 %all-gather.2.cloned.1.call-start = ((), (), s32[]{:S(2)}) async-start(), calls=%async_computation.4 | async-start | bytes 8650752 | tf_op jit(solution)/shard_map/all_gather | solution.py:68
  36.2 10.2 %all-to-all-start.2 = ((bf16[32,16,128]{2,0,1:T(8,128)(2,1)}), bf16[32,16,128]{2,0,1:T(8,128)(2,1)S(1)}, u32[]{:S(2)}, u32[]{:S(2)}) async-start(bf16[32,16,128]{2,0,1:T(8,128)(2,1)} %copy_bitcast_fusion.1), calls=%async_computation.2 | async-start | bytes 262144 | tf_op jit(solution)/shard_map/all_to_all | solution.py:14
Sparse Core Ops, SparseCore 0:
  34.8 184.0 all-gather.1
where the time goes:
time: 323 us; the launch traced here: 322 us
  waiting for transfers between devices  181 us (56%)
  matrix products  35.3 us (11%)
  local copies, waits for them, and re-layouts  31.3 us (10%)
  blocking collectives  27.9 us (9%)
  between operations  15.1 us (5%)
  starting transfers between devices  14.2 us (4%)
  other arithmetic  10.9 us (3%)
  loops' own time  6.01 us (2%)
    all_gather x1, waiting for transfers between devices, per_device(): kv_piece = lax.all_gather(kv_pair, 'blk', axis=1, tiled=True)  172 us
    dot_general x8, matrix products, block_update(): jnp.einsum('hqk,khd->qhd', probs.astype(jnp.bfloat16), value_three, prefe...  19 us
    all_to_all x1, blocking collectives, per_device(): lax.all_to_all(output, 'uly', split_axis=0, concat_axis=1, tiled=True)  18.6 us
    dot_general x8, matrix products, block_update(): jnp.einsum('qhd,khd->hqk', query_three, key_three, preferred_element_type...  16.3 us
    gather x8, local copies, waits for them, and re-layouts, block_update(): key_frames = jnp.take(frame_order, key_tile_ids // query_tiles)  10.5 us
    all_to_all x1, starting transfers between devices, per_device(): lax.all_to_all(keys, 'uly', split_axis=1, concat_axis=0, tiled=True)  10.2 us
    reduce_sum x8, other arithmetic, block_update(): new_sum = running_sum * factor + jnp.sum(probs, axis=-1)  9.34 us
    all_to_all x1, blocking collectives, per_device(): lax.all_to_all(values, 'uly', split_axis=1, concat_axis=0, tiled=True)  9.3 us
  transfers between devices with their start and end apart: 3, of which 3 were waited for; matrix products, arithmetic and copies ran while one was open for 1% of the time, Pallas kernels for 0%

commit v1 on v0

v1 whole, which is shorter than its diff:
```python
import functools
import math

import jax
import jax.numpy as jnp
from jax import lax
from jax.experimental import pallas as pl
from jax.experimental.pallas import tpu as pltpu
from jax.sharding import PartitionSpec as P

HD = 128
CH = 32
NZ = 16
GZ = 4
STEPS = NZ // GZ
MASKED = -1e30
SCALE = math.log2(math.e) / math.sqrt(HD)
MESH = pl.DeviceIdType.MESH
F32 = jnp.float32
BF16 = jnp.bfloat16


def kernel(
    q_ref, k_ref, v_ref, bias_ref, out_ref,
    qbuf, kv, acc, top, osend, lsend, orecv, lrecv, oown, lown, zsend,
    q_sent, k_sent, v_sent, q_got, kv_got, y_sent, y_got,
    x_sent, x_got, sib_got, o_sent, l_sent, o_got, l_got, r_sent, r_got,
):
    b, u = lax.axis_index("blk"), lax.axis_index("uly")
    z, xh = b // 2, b % 2
    y, xl, c = u // 4, (u // 2) % 2, u % 2
    x = xh * 2 + xl
    ahead, behind, opposite = (x + 1 + 2 * c) % 4, (x + 3 - 2 * c) % 4, (x + 2) % 4

    def dev(z2=z, x2=x, y2=y, c2=c):
        return {"blk": z2 * 2 + x2 // 2, "uly": y2 * 4 + (x2 % 2) * 2 + c2}

    def remote(src, dst, send, recv, device):
        return pltpu.make_async_remote_copy(
            src_ref=src, dst_ref=dst, send_sem=send, recv_sem=recv,
            device_id=device, device_id_type=MESH,
        )

    def wait_bytes(ref, sem):
        pltpu.make_async_copy(ref, ref, sem).wait()

    def far(i):
        mag = (i + 1) // 2
        return (z + NZ + (2 * (i % 2) - 1) * mag) % NZ

    barrier = pltpu.get_barrier_semaphore()

    def greet(i, carry):
        pl.semaphore_signal(barrier, inc=1, device_id=dev(z2=far(i)), device_id_type=MESH)
        return carry

    lax.fori_loop(1, NZ, greet, 0)
    for dy in range(1, 4):
        pl.semaphore_signal(barrier, inc=1, device_id=dev(y2=(y + dy) % 4), device_id_type=MESH)
    pl.semaphore_signal(barrier, inc=1, device_id=dev(x2=ahead), device_id_type=MESH)
    pl.semaphore_signal(barrier, inc=1, device_id=dev(x2=behind), device_id_type=MESH)
    pl.semaphore_signal(barrier, inc=1, device_id=dev(c2=1 - c), device_id_type=MESH)
    pl.semaphore_wait(barrier, NZ - 1 + 3 + 2 + 1)

    zslot = (z % 2) * (NZ // 2) + z // 2

    def cols(ref, h):
        return ref.at[:, pl.ds(pl.multiple_of(h * HD, HD), HD)]

    q_dst = qbuf.at[y, zslot, :, pl.ds(0, HD)]
    k_dst = kv.at[z, xh, 0, xl, c, :, pl.ds(0, HD)]
    v_dst = kv.at[z, xh, 1, xl, c, :, pl.ds(0, HD)]
    pltpu.make_async_copy(cols(q_ref, z), q_dst, q_got).start()
    pltpu.make_async_copy(cols(k_ref, z), k_dst, kv_got.at[z // GZ]).start()
    pltpu.make_async_copy(cols(v_ref, z), v_dst, kv_got.at[z // GZ]).start()

    def q_copy(i):
        h = far(i)
        return remote(cols(q_ref, h), q_dst, q_sent.at[i], q_got, dev(z2=h))

    def k_copy(i):
        h = far(i)
        return remote(cols(k_ref, h), k_dst, k_sent.at[i], kv_got.at[z // GZ], dev(z2=h))

    def v_copy(i):
        h = far(i)
        return remote(cols(v_ref, h), v_dst, v_sent.at[i], kv_got.at[z // GZ], dev(z2=h))

    def start_q(i, carry):
        q_copy(i).start()
        return carry

    def start_kv(i, carry):
        k_copy(i).start()
        v_copy(i).start()
        return carry

    lax.fori_loop(1, NZ, start_q, 0)
    lax.fori_loop(1, NZ, start_kv, 0)

    lane = lax.broadcasted_iota(jnp.int32, (4 * CH, HD), 1)

    def fill_kv(i, carry):
        zz, hh = i // 2, i % 2
        hot = jnp.where(lane == i, 1.0, 0.0).astype(BF16).reshape(2, 2, CH, HD)
        kv[zz, hh, 0, :, :, :, HD:] = hot
        kv[zz, hh, 1, :, :, :, HD:] = jnp.ones((2, 2, CH, HD), BF16)
        return carry

    lax.fori_loop(0, 2 * NZ, fill_kv, 0)
    for qt in range(4):
        for s in range(NZ):
            row = bias_ref[qt * NZ + s : qt * NZ + s + 1, :]
            qbuf[qt, s, :, HD:] = jnp.broadcast_to(row, (CH, HD)).astype(BF16)

    def zero(i, carry):
        qt, s = i // NZ, i % NZ
        acc[qt, s] = jnp.zeros((CH, 2 * HD), F32)
        top[qt, s] = jnp.full((CH, HD), -3e38, F32)
        return carry

    lax.fori_loop(0, 4 * NZ, zero, 0)

    q_slab = qbuf.at[y, :, :, pl.ds(0, HD)]
    wait_bytes(q_slab, q_got)
    y_copies = [
        remote(q_slab, q_slab, y_sent.at[dy - 1], y_got.at[dy - 1], dev(y2=(y + dy) % 4))
        for dy in range(1, 4)
    ]
    for copy in y_copies:
        copy.start()

    zq = z // GZ
    order = [zq, (zq + 1) % STEPS, (zq + 3) % STEPS, (zq + 2) % STEPS]

    def part(g, x2, c2=c):
        return kv.at[pl.ds(g * GZ, GZ), x2 // 2, :, x2 % 2, c2, :, pl.ds(0, HD)]

    x_copies = []

    def push(n, slot, g, x2, recv, device):
        ref = part(g, x2)
        copy = remote(ref, ref, x_sent.at[n, slot], recv, device)
        copy.start()
        x_copies.append(copy)

    sib = dev(c2=1 - c)

    def stage1(n):
        g = order[n]
        wait_bytes(part(g, x), kv_got.at[g])
        push(n, 0, g, x, x_got.at[n, 0], dev(x2=ahead))
        push(n, 1, g, x, x_got.at[n, 1], dev(x2=behind))
        push(n, 2, g, x, sib_got.at[n], sib)

    def stage2(n):
        g = order[n]
        wait_bytes(part(g, behind), x_got.at[n, 0])
        push(n, 3, g, behind, x_got.at[n, 2], dev(x2=ahead))
        push(n, 4, g, behind, sib_got.at[n], sib)
        wait_bytes(part(g, ahead), x_got.at[n, 1])
        push(n, 5, g, ahead, sib_got.at[n], sib)

    def stage3(n):
        g = order[n]
        wait_bytes(part(g, opposite), x_got.at[n, 2])
        push(n, 6, g, opposite, sib_got.at[n], sib)

    def stage4(n):
        g = order[n]
        wait_bytes(kv.at[pl.ds(g * GZ, GZ), :, :, :, 1 - c, :, pl.ds(0, HD)], sib_got.at[n])

    HB = NZ // 2
    ROWS = HB * CH

    def attend(n, qt, j):
        g = order[n]
        rows = pl.ds(j * HB, HB)
        qq = qbuf[qt, rows].reshape(ROWS, 2 * HD)
        kk = kv[pl.ds(g * GZ, GZ), :, 0].reshape(GZ * 8 * CH, 2 * HD)
        vv = kv[pl.ds(g * GZ, GZ), :, 1].reshape(GZ * 8 * CH, 2 * HD)
        s = lax.dot_general(qq, kk, (((1,), (1,)), ((), ())), preferred_element_type=F32)
        old = top[qt, rows].reshape(ROWS, HD)
        new = jnp.maximum(old, jnp.max(s, axis=1, keepdims=True))
        p = jnp.exp2((s - new[:, :1]) * SCALE).astype(BF16)
        pv = jnp.dot(p, vv, preferred_element_type=F32)
        fade = jnp.exp2((old - new) * SCALE)
        total = acc[qt, rows].reshape(ROWS, 2 * HD)
        total = jnp.concatenate([total[:, :HD] * fade, total[:, HD:] * fade], axis=1) + pv
        return total, new

    def attend_store(n, qt, j):
        total, new = attend(n, qt, j)
        acc[qt, pl.ds(j * HB, HB)] = total.reshape(HB, CH, 2 * HD)
        top[qt, pl.ds(j * HB, HB)] = new.reshape(HB, CH, HD)

    def blocks(n, lo, hi):
        def one(i, carry):
            attend_store(n, i // 2, i % 2)
            return carry

        lax.fori_loop(lo, hi, one, 0)

    stage1(0)
    stage2(0)
    stage3(0)
    for dy in range(1, 4):
        y_copies[dy - 1].wait_recv()
    stage4(0)
    for n in range(STEPS - 1):
        stage1(n + 1)
        blocks(n, 0, 4)
        stage2(n + 1)
        blocks(n, 4, 8)
        stage3(n + 1)
        stage4(n + 1)

    eye = (
        lax.broadcasted_iota(jnp.int32, (HD, HD), 0) == lax.broadcasted_iota(jnp.int32, (HD, HD), 1)
    )

    def o_copy(i):
        d, j = i // 2, i % 2
        return remote(
            osend.at[d, j], orecv.at[d, j], o_sent.at[d, j], o_got.at[d, j],
            dev(y2=(y + d + 1) % 4),
        )

    def l_copy(i):
        d, j = i // 2, i % 2
        return remote(
            lsend.at[d, j], lrecv.at[d, j], l_sent.at[d, j], l_got.at[d, j],
            dev(y2=(y + d + 1) % 4),
        )

    def finish(i):
        total, new = attend(STEPS - 1, (y + i // 2 + 1) % 4, i % 2)
        summed = total[:, HD:]
        return total[:, :HD] / summed, new * SCALE + jnp.log2(summed)

    def last(i, carry):
        o, lse = finish(i)
        d, j = i // 2, i % 2
        osend[d, j] = o.astype(BF16).reshape(HB, CH, HD)
        lsend[d, j] = jnp.sum(
            jnp.where(eye[None], lse.reshape(ROWS // HD, HD, HD), 0.0), axis=1
        )
        o_copy(i).start()
        l_copy(i).start()
        return carry

    lax.fori_loop(0, 6, last, 0)

    def last_own(j, carry):
        o, lse = finish(6 + j)
        oown[j] = o
        lown[j] = lse
        return carry

    lax.fori_loop(0, 2, last_own, 0)

    r_dst = cols(out_ref, z)

    def r_copy(j, i):
        z2 = 2 * i + j
        return remote(zsend.at[j, i], r_dst, r_sent.at[j, i], r_got, dev(z2=z2))

    def combine(j, carry):
        parts = [oown[j]]
        weights = [lown[j]]
        for d in range(3):
            o_copy(2 * d + j).wait_recv()
            l_copy(2 * d + j).wait_recv()
            stat = lrecv[d, j]
            wide = jnp.sum(
                jnp.where(eye[None], jnp.broadcast_to(stat[:, None, :], (ROWS // HD, HD, HD)), 0.0),
                axis=2, keepdims=True,
            )
            weights.append(jnp.broadcast_to(wide, (ROWS // HD, HD, HD)).reshape(ROWS, HD))
            parts.append(orecv[d, j].reshape(ROWS, HD).astype(F32))
        high = functools.reduce(jnp.maximum, weights)
        weights = [jnp.exp2(w - high) for w in weights]
        mixed = sum(w * o for w, o in zip(weights, parts)) / sum(weights)
        zsend[j] = mixed.astype(BF16).reshape(HB, CH, HD)

        def home(i, carry2):
            z2 = 2 * i + j

            @pl.when(z2 != z)
            def _():
                r_copy(j, i).start()

            @pl.when(z2 == z)
            def _():
                pltpu.make_async_copy(zsend.at[j, i], r_dst, r_got).start()

            return carry2

        lax.fori_loop(0, HB, home, 0)
        return carry

    lax.fori_loop(0, 2, combine, 0)
    wait_bytes(out_ref, r_got)

    def drain_z(i, carry):
        q_copy(i).wait_send()
        k_copy(i).wait_send()
        v_copy(i).wait_send()
        return carry

    lax.fori_loop(1, NZ, drain_z, 0)
    for copy in y_copies + x_copies:
        copy.wait_send()

    def drain_o(i, carry):
        o_copy(i).wait_send()
        l_copy(i).wait_send()
        return carry

    lax.fori_loop(0, 6, drain_o, 0)

    def drain_r(i, carry):
        @pl.when(i != z)
        def _():
            r_copy(i % 2, i // 2).wait_send()

        return carry

    lax.fori_loop(0, NZ, drain_r, 0)


def attention(queries, keys, values, bias):
    dma = pltpu.SemaphoreType.DMA
    vmem = pl.BlockSpec(memory_space=pltpu.VMEM)
    return pl.pallas_call(
        kernel,
        out_shape=jax.ShapeDtypeStruct(queries.shape, BF16),
        in_specs=[vmem] * 4,
        out_specs=vmem,
        scratch_shapes=[
            pltpu.VMEM((4, NZ, CH, 2 * HD), BF16),
            pltpu.VMEM((NZ, 2, 2, 2, 2, CH, 2 * HD), BF16),
            pltpu.VMEM((4, NZ, CH, 2 * HD), F32),
            pltpu.VMEM((4, NZ, CH, HD), F32),
            pltpu.VMEM((3, 2, NZ // 2, CH, HD), BF16),
            pltpu.VMEM((3, 2, 2, HD), F32),
            pltpu.VMEM((3, 2, NZ // 2, CH, HD), BF16),
            pltpu.VMEM((3, 2, 2, HD), F32),
            pltpu.VMEM((2, NZ // 2 * CH, HD), F32),
            pltpu.VMEM((2, NZ // 2 * CH, HD), F32),
            pltpu.VMEM((2, NZ // 2, CH, HD), BF16),
            dma((NZ,)), dma((NZ,)), dma((NZ,)),
            dma, dma((STEPS,)),
            dma((3,)), dma((3,)),
            dma((STEPS, 7)), dma((STEPS, 3)), dma((STEPS,)),
            dma((3, 2)), dma((3, 2)), dma((3, 2)), dma((3, 2)),
            dma((2, NZ // 2)), dma,
        ],
        compiler_params=pltpu.CompilerParams(
            collective_id=0, has_side_effects=True, vmem_limit_bytes=40 * 2**20
        ),
        name="attention",
    )(queries, keys, values, bias)


def per_device(queries, keys, values, tile_mask, frame_order):
    b, u = lax.axis_index("blk"), lax.axis_index("uly")
    xh, y = b % 2, u // 4
    order = frame_order.reshape(NZ, 2)
    mine = lax.dynamic_index_in_dim(order, xh, 1, keepdims=False)
    mine = jnp.transpose(mine.reshape(NZ // 2, 2)).reshape(NZ)
    columns = lax.dynamic_index_in_dim(tile_mask, y, 3, keepdims=False)
    chosen = columns[mine][:, frame_order]
    bias = jnp.where(jnp.transpose(chosen, (2, 0, 1)) > 0, 0.0, MASKED)
    bias = jnp.pad(bias.reshape(4 * NZ, 2 * NZ), ((0, 0), (0, HD - 2 * NZ)))
    return attention(queries, keys, values, bias)


def solution(mesh):
    rows = P(("blk", "uly"), None)
    return jax.shard_map(
        per_device,
        mesh=mesh,
        in_specs=(rows, rows, rows, P(), P()),
        out_specs=rows,
        check_vma=False,
    )
```

time: 323 us -> 90.6 us (0.28)
  the two profiles are of different devices: /device:TPU:1 before, /device:TPU:40 now
where the time goes in v1:
time: 90.6 us; the launch traced here: 90.5 us
  Pallas kernels  86.2 us (95%)
  local copies, waits for them, and re-layouts  4.16 us (5%)
    pallas_call x1, Pallas kernels, attention(): pl.pallas_call(kernel, out_shape=jax.ShapeDtypeStruct(queries.shape, BF16...  86.2 us
    unnamed x11, local copies, waits for them, and re-layouts  2.22 us

profile of v1, /device:TPU:40, one launch (start us, length us, event | category | flops | bytes accessed | tf_op | source)
XLA Modules:
  0.0 90.5 jit_solution(1116520554006769787)
XLA Ops:
  0.0 0.0 copy-start
  0.0 0.0 copy-start.4
  0.0 0.7 copy-done.4
  0.7 0.1 reshape.41
  0.8 0.2 dynamic-slice_reduce_fusion
  1.0 0.1 reshape.42
  1.1 0.1 copy.9
  1.1 0.1 reshape.43
  1.3 0.0 copy-done
  1.3 0.1 constant_dynamic-slice_fusion
  1.3 0.6 gather_fusion
  1.9 0.1 copy.10
  2.0 0.0 copy-start.3
  2.0 0.6 gather_fusion.1
  2.6 0.0 copy-start.1
  2.7 0.0 copy-start.2
  2.7 0.1 copy.11
  2.8 0.1 copy-done.3
  2.9 0.6 copy-done.1
  3.6 0.1 copy-done.2
  3.6 86.2 %attention.1 = bf16[32,2048]{1,0:T(8,128)(2,1)S(1)} custom-call(bf16[32,2048]{1,0:T(8,128)(2,1)S(1)} %copy-done.1, bf16[32,2048]{1,0:T(8,128)(2,1)S(1)} %copy-done.2, bf16[32,2048]{1,0:T(8,128)(2,1)S(1)} %copy-done.3, f32[64,128]{1,0:T(8,128)S(1)} %pad.4.bias_ref), custom_call_target="tpu_custom_call" | custom-call | tf_op jit(solution)/shard_map/attention/pallas_call | solution.py:335
  89.8 0.7 copy.13
  (6 shorter events, 0.1 us)
Async XLA Ops:
  0.0 1.3 %copy-start = (s32[32,32,4,4]{1,3,2,0:T(4,128)S(1)}, s32[32,32,4,4]{1,3,2,0:T(4,128)}, u32[]{:S(2)}) copy-start(s32[32,32,4,4]{1,3,2,0:T(4,128)} %param.8) | copy-start | bytes 196612
  0.0 0.7 copy-start.4
  2.0 0.9 %copy-start.3 = (bf16[32,2048]{1,0:T(8,128)(2,1)S(1)}, bf16[32,2048]{1,0:T(8,128)(2,1)}, u32[]{:S(2)}) copy-start(bf16[32,2048]{1,0:T(8,128)(2,1)} %v_ref.1) | copy-start | bytes 393220
  2.6 0.9 %copy-start.1 = (bf16[32,2048]{1,0:T(8,128)(2,1)S(1)}, bf16[32,2048]{1,0:T(8,128)(2,1)}, u32[]{:S(2)}) copy-start(bf16[32,2048]{1,0:T(8,128)(2,1)} %q_ref.1) | copy-start | bytes 393220
  2.7 1.0 %copy-start.2 = (bf16[32,2048]{1,0:T(8,128)(2,1)S(1)}, bf16[32,2048]{1,0:T(8,128)(2,1)}, u32[]{:S(2)}) copy-start(bf16[32,2048]{1,0:T(8,128)(2,1)} %k_ref.1) | copy-start | bytes 393220

commit v2 on v1

v2 whole, which is shorter than its diff:
```python
import functools
import math

import jax
import jax.numpy as jnp
from jax import lax
from jax.experimental import pallas as pl
from jax.experimental.pallas import tpu as pltpu
from jax.sharding import PartitionSpec as P

HD = 128
CH = 32
NZ = 16
GZ = 4
STEPS = NZ // GZ
MASKED = -1e30
SCALE = math.log2(math.e) / math.sqrt(HD)
MESH = pl.DeviceIdType.MESH
F32 = jnp.float32
BF16 = jnp.bfloat16


def kernel(
    q_ref, k_ref, v_ref, mask_ref, order_ref, out_ref,
    mask, frames, qbuf, kv, acc, top, osend, lsend, orecv, lrecv, oown, lown, zsend,
    q_sent, k_sent, v_sent, q_got, kv_got, y_sent, y_got,
    x_sent, x_got, sib_got, o_sent, l_sent, o_got, l_got, r_sent, r_got, in_got,
):
    b, u = lax.axis_index("blk"), lax.axis_index("uly")
    z, xh = b // 2, b % 2
    y, xl, c = u // 4, (u // 2) % 2, u % 2
    x = xh * 2 + xl
    ahead, behind, opposite = (x + 1 + 2 * c) % 4, (x + 3 - 2 * c) % 4, (x + 2) % 4

    def dev(z2=z, x2=x, y2=y, c2=c):
        return {"blk": z2 * 2 + x2 // 2, "uly": y2 * 4 + (x2 % 2) * 2 + c2}

    def remote(src, dst, send, recv, device):
        return pltpu.make_async_remote_copy(
            src_ref=src, dst_ref=dst, send_sem=send, recv_sem=recv,
            device_id=device, device_id_type=MESH,
        )

    def wait_bytes(ref, sem):
        pltpu.make_async_copy(ref, ref, sem).wait()

    def plane(i):
        return lax.rem(z + NZ + (2 * (i % 2) - 1) * ((i + 1) // 2), NZ)

    barrier = pltpu.get_barrier_semaphore()
    partners = [dev(z2=plane(i)) for i in range(NZ - 1, 0, -1)]
    partners += [dev(y2=lax.rem(y + dy, 4)) for dy in (2, 1, 3)]
    partners += [dev(x2=ahead), dev(x2=behind), dev(c2=1 - c)]
    for partner in partners:
        pl.semaphore_signal(barrier, inc=1, device_id=partner, device_id_type=MESH)
    mask_copy = pltpu.make_async_copy(mask_ref, mask, in_got.at[0])
    frames_copy = pltpu.make_async_copy(order_ref, frames, in_got.at[1])
    mask_copy.start()
    frames_copy.start()
    pl.semaphore_wait(barrier, len(partners))

    zslot = (z % 2) * (NZ // 2) + z // 2

    def cols(ref, h):
        return ref.at[:, pl.ds(pl.multiple_of(h * HD, HD), HD)]

    q_dst = qbuf.at[y, zslot, :, pl.ds(0, HD)]
    k_dst = kv.at[z, xh, 0, xl, c, :, pl.ds(0, HD)]
    v_dst = kv.at[z, xh, 1, xl, c, :, pl.ds(0, HD)]
    pltpu.make_async_copy(cols(q_ref, z), q_dst, q_got).start()
    pltpu.make_async_copy(cols(k_ref, z), k_dst, kv_got.at[z // GZ]).start()
    pltpu.make_async_copy(cols(v_ref, z), v_dst, kv_got.at[z // GZ]).start()

    def q_copy(i):
        h = plane(i)
        return remote(cols(q_ref, h), q_dst, q_sent.at[i], q_got, dev(z2=h))

    def k_copy(i):
        h = plane(i)
        return remote(cols(k_ref, h), k_dst, k_sent.at[i], kv_got.at[z // GZ], dev(z2=h))

    def v_copy(i):
        h = plane(i)
        return remote(cols(v_ref, h), v_dst, v_sent.at[i], kv_got.at[z // GZ], dev(z2=h))

    def start_q(i, carry):
        q_copy(i).start()
        return carry

    def start_kv(i, carry):
        k_copy(i).start()
        v_copy(i).start()
        return carry

    lax.fori_loop(1, NZ, start_q, 0)
    lax.fori_loop(1, NZ, start_kv, 0)

    lane = lax.broadcasted_iota(jnp.int32, (4 * CH, HD), 1)
    mask_copy.wait()
    frames_copy.wait()

    def fill_kv(i, carry):
        zz, hh = i // 2, i % 2
        hot = jnp.where(lane == frames[i], 1.0, 0.0).astype(BF16).reshape(2, 2, CH, HD)
        kv[zz, hh, 0, :, :, :, HD:] = hot
        kv[zz, hh, 1, :, :, :, HD:] = jnp.ones((2, 2, CH, HD), BF16)
        return carry

    lax.fori_loop(0, 2 * NZ, fill_kv, 0)

    def fill_q(zz, carry):
        s = (zz % 2) * (NZ // 2) + zz // 2
        rows = mask[frames[2 * zz + xh], :, y, :]
        rows = jnp.where(rows > 0, 0.0, MASKED)
        for qt in range(4):
            qbuf[qt, s, :, HD:] = jnp.zeros((CH, HD), BF16)
            wide = jnp.broadcast_to(rows[qt : qt + 1], (CH, 2 * NZ)).astype(BF16)
            qbuf[qt, s, :, HD : HD + 2 * NZ] = wide
        return carry

    lax.fori_loop(0, NZ, fill_q, 0)

    def zero(i, carry):
        qt, s = i // NZ, i % NZ
        acc[qt, s] = jnp.zeros((CH, 2 * HD), F32)
        top[qt, s] = jnp.full((CH, HD), -3e38, F32)
        return carry

    lax.fori_loop(0, 4 * NZ, zero, 0)

    q_slab = qbuf.at[y, :, :, pl.ds(0, HD)]
    wait_bytes(q_slab, q_got)
    y_copies = [
        remote(q_slab, q_slab, y_sent.at[dy - 1], y_got.at[dy - 1], dev(y2=(y + dy) % 4))
        for dy in range(1, 4)
    ]
    for copy in y_copies:
        copy.start()

    zq = z // GZ

    def group(n):
        return lax.rem(zq + n + (n // 2) * (1 - 2 * (n % 2)), STEPS)

    def part(g, x2, c2=c):
        return kv.at[pl.ds(g * GZ, GZ), x2 // 2, :, x2 % 2, c2, :, pl.ds(0, HD)]

    def push(n, slot, x2, recv, device):
        ref = part(group(n), x2)
        return remote(ref, ref, x_sent.at[n, slot], recv, device)

    sib = dev(c2=1 - c)

    def pushes(n):
        return [
            push(n, 0, x, x_got.at[n, 0], dev(x2=ahead)),
            push(n, 1, x, x_got.at[n, 1], dev(x2=behind)),
            push(n, 2, x, sib_got.at[n], sib),
            push(n, 3, behind, x_got.at[n, 2], dev(x2=ahead)),
            push(n, 4, behind, sib_got.at[n], sib),
            push(n, 5, ahead, sib_got.at[n], sib),
            push(n, 6, opposite, sib_got.at[n], sib),
        ]

    def stage1(n):
        g = group(n)
        wait_bytes(part(g, x), kv_got.at[g])
        for copy in pushes(n)[:3]:
            copy.start()

    def stage2(n):
        g = group(n)
        wait_bytes(part(g, behind), x_got.at[n, 0])
        for copy in pushes(n)[3:5]:
            copy.start()
        wait_bytes(part(g, ahead), x_got.at[n, 1])
        pushes(n)[5].start()

    def stage3(n):
        g = group(n)
        wait_bytes(part(g, opposite), x_got.at[n, 2])
        pushes(n)[6].start()

    def stage4(n):
        g = group(n)
        wait_bytes(kv.at[pl.ds(g * GZ, GZ), :, :, :, 1 - c, :, pl.ds(0, HD)], sib_got.at[n])

    HB = NZ // 2
    ROWS = HB * CH

    def attend(n, qt, j):
        g = group(n)
        rows = pl.ds(j * HB, HB)
        qq = qbuf[qt, rows].reshape(ROWS, 2 * HD)
        kk = kv[pl.ds(g * GZ, GZ), :, 0].reshape(GZ * 8 * CH, 2 * HD)
        vv = kv[pl.ds(g * GZ, GZ), :, 1].reshape(GZ * 8 * CH, 2 * HD)
        s = lax.dot_general(qq, kk, (((1,), (1,)), ((), ())), preferred_element_type=F32)
        old = top[qt, rows].reshape(ROWS, HD)
        new = jnp.maximum(old, jnp.max(s, axis=1, keepdims=True))
        p = jnp.exp2((s - new[:, :1]) * SCALE).astype(BF16)
        pv = jnp.dot(p, vv, preferred_element_type=F32)
        fade = jnp.exp2((old - new) * SCALE)
        total = acc[qt, rows].reshape(ROWS, 2 * HD)
        total = jnp.concatenate([total[:, :HD] * fade, total[:, HD:] * fade], axis=1) + pv
        return total, new

    def attend_store(n, qt, j):
        total, new = attend(n, qt, j)
        acc[qt, pl.ds(j * HB, HB)] = total.reshape(HB, CH, 2 * HD)
        top[qt, pl.ds(j * HB, HB)] = new.reshape(HB, CH, HD)

    stage1(0)
    stage2(0)
    stage3(0)
    for dy in range(1, 4):
        y_copies[dy - 1].wait_recv()
    stage4(0)

    def step(n, carry):
        stage1(n + 1)
        for qt in range(4):
            attend_store(n, qt, 0)
        stage2(n + 1)
        for qt in range(4):
            attend_store(n, qt, 1)
        stage3(n + 1)
        stage4(n + 1)
        return carry

    lax.fori_loop(0, STEPS - 1, step, 0)

    eye = (
        lax.broadcasted_iota(jnp.int32, (HD, HD), 0) == lax.broadcasted_iota(jnp.int32, (HD, HD), 1)
    )

    def o_copy(d, j):
        return remote(
            osend.at[d, j], orecv.at[d, j], o_sent.at[d, j], o_got.at[d, j],
            dev(y2=lax.rem(y + d + 1, 4)),
        )

    def l_copy(d, j):
        return remote(
            lsend.at[d, j], lrecv.at[d, j], l_sent.at[d, j], l_got.at[d, j],
            dev(y2=lax.rem(y + d + 1, 4)),
        )

    def last(j, carry):
        for d in (1, 0, 2, 3):
            total, new = attend(STEPS - 1, lax.rem(y + d + 1, 4), j)
            summed = total[:, HD:]
            o = total[:, :HD] / summed
            lse = new * SCALE + jnp.log2(summed)
            if d == 3:
                oown[j] = o
                lown[j] = lse
            else:
                osend[d, j] = o.astype(BF16).reshape(HB, CH, HD)
                lsend[d, j] = jnp.sum(
                    jnp.where(eye[None], lse.reshape(ROWS // HD, HD, HD), 0.0), axis=1
                )
        for d in (1, 0, 2):
            o_copy(d, j).start()
            l_copy(d, j).start()
        return carry

    lax.fori_loop(0, 2, last, 0)

    r_dst = cols(out_ref, z)

    def r_copy(j, i):
        z2 = 2 * i + j
        return remote(zsend.at[j, i], r_dst, r_sent.at[j, i], r_got, dev(z2=z2))

    def combine(j, carry):
        parts = [oown[j]]
        weights = [lown[j]]
        for d in range(3):
            o_copy(d, j).wait_recv()
            l_copy(d, j).wait_recv()
            stat = lrecv[d, j]
            wide = jnp.sum(
                jnp.where(eye[None], jnp.broadcast_to(stat[:, None, :], (ROWS // HD, HD, HD)), 0.0),
                axis=2, keepdims=True,
            )
            weights.append(jnp.broadcast_to(wide, (ROWS // HD, HD, HD)).reshape(ROWS, HD))
            parts.append(orecv[d, j].reshape(ROWS, HD).astype(F32))
        high = functools.reduce(jnp.maximum, weights)
        weights = [jnp.exp2(w - high) for w in weights]
        mixed = sum(w * o for w, o in zip(weights, parts)) / sum(weights)
        zsend[j] = mixed.astype(BF16).reshape(HB, CH, HD)

        def home(i, carry2):
            z2 = 2 * i + j

            @pl.when(z2 != z)
            def _():
                r_copy(j, i).start()

            @pl.when(z2 == z)
            def _():
                pltpu.make_async_copy(zsend.at[j, i], r_dst, r_got).start()

            return carry2

        lax.fori_loop(0, HB, home, 0)
        return carry

    lax.fori_loop(0, 2, combine, 0)
    wait_bytes(out_ref, r_got)

    def drain_z(i, carry):
        q_copy(i).wait_send()
        k_copy(i).wait_send()
        v_copy(i).wait_send()
        return carry

    lax.fori_loop(1, NZ, drain_z, 0)
    for copy in y_copies:
        copy.wait_send()

    def drain_x(n, carry):
        for copy in pushes(n):
            copy.wait_send()
        return carry

    lax.fori_loop(0, STEPS, drain_x, 0)

    def drain_o(j, carry):
        for d in range(3):
            o_copy(d, j).wait_send()
            l_copy(d, j).wait_send()
        return carry

    lax.fori_loop(0, 2, drain_o, 0)

    def drain_r(i, carry):
        @pl.when(i != z)
        def _():
            r_copy(i % 2, i // 2).wait_send()

        return carry

    lax.fori_loop(0, NZ, drain_r, 0)


def attention(queries, keys, values, tile_mask, frame_order):
    dma = pltpu.SemaphoreType.DMA
    hbm = pl.BlockSpec(memory_space=pl.ANY)
    return pl.pallas_call(
        kernel,
        out_shape=jax.ShapeDtypeStruct(queries.shape, BF16),
        in_specs=[hbm] * 5,
        out_specs=hbm,
        scratch_shapes=[
            pltpu.VMEM((2 * NZ, 4, 4, 2 * NZ), jnp.int32),
            pltpu.SMEM((2 * NZ,), jnp.int32),
            pltpu.VMEM((4, NZ, CH, 2 * HD), BF16),
            pltpu.VMEM((NZ, 2, 2, 2, 2, CH, 2 * HD), BF16),
            pltpu.VMEM((4, NZ, CH, 2 * HD), F32),
            pltpu.VMEM((4, NZ, CH, HD), F32),
            pltpu.VMEM((3, 2, NZ // 2, CH, HD), BF16),
            pltpu.VMEM((3, 2, 2, HD), F32),
            pltpu.VMEM((3, 2, NZ // 2, CH, HD), BF16),
            pltpu.VMEM((3, 2, 2, HD), F32),
            pltpu.VMEM((2, NZ // 2 * CH, HD), F32),
            pltpu.VMEM((2, NZ // 2 * CH, HD), F32),
            pltpu.VMEM((2, NZ // 2, CH, HD), BF16),
            dma((NZ,)), dma((NZ,)), dma((NZ,)),
            dma, dma((STEPS,)),
            dma((3,)), dma((3,)),
            dma((STEPS, 7)), dma((STEPS, 3)), dma((STEPS,)),
            dma((3, 2)), dma((3, 2)), dma((3, 2)), dma((3, 2)),
            dma((2, NZ // 2)), dma, dma((2,)),
        ],
        compiler_params=pltpu.CompilerParams(
            collective_id=0, has_side_effects=True, vmem_limit_bytes=56 * 2**20
        ),
        name="attention",
    )(queries, keys, values, tile_mask, frame_order)


def per_device(queries, keys, values, tile_mask, frame_order):
    by_key = jnp.transpose(tile_mask, (0, 2, 3, 1))
    return attention(queries, keys, values, by_key, frame_order)


def solution(mesh):
    rows = P(("blk", "uly"), None)
    return jax.shard_map(
        per_device,
        mesh=mesh,
        in_specs=(rows, rows, rows, P(), P()),
        out_specs=rows,
        check_vma=False,
    )
```

time: 90.6 us -> 80.9 us (0.89)
  the two profiles are of different devices: /device:TPU:40 before, /device:TPU:1 now
where the time goes in v2:
time: 80.9 us; the launch traced here: 79.8 us
  Pallas kernels  78.2 us (97%)
  local copies, waits for them, and re-layouts  1.57 us (2%)
    pallas_call x1, Pallas kernels, attention(): pl.pallas_call(kernel, out_shape=jax.ShapeDtypeStruct(queries.shape, BF16...  78.2 us

profile of v2, /device:TPU:1, one launch (start us, length us, event | category | flops | bytes accessed | tf_op | source)
XLA Modules:
  0.0 79.8 jit_solution(18018620661360775601)
XLA Ops:
  0.0 78.2 %attention.1 = bf16[32,2048]{1,0:T(8,128)(2,1)} custom-call(bf16[32,2048]{1,0:T(8,128)(2,1)} %q_ref.1, bf16[32,2048]{1,0:T(8,128)(2,1)} %k_ref.1, bf16[32,2048]{1,0:T(8,128)(2,1)} %v_ref.1, s32[32,4,4,32]{3,2,1,0:T(4,128)} %bitcast.1, s32[32]{0:T(128)} %order_ref.1), custom_call_target="tpu_custom_call" | custom-call | tf_op jit(solution)/shard_map/attention/pallas_call | solution.py:350
  78.2 1.6 %copy.7 = bf16[32,2048]{1,0:T(8,128)(2,1)} copy(bf16[32,2048]{1,0:T(8,128)(2,1)} %attention.1) | data formatting | bytes 262144

commit v3 on v2

v3 whole, which is shorter than its diff:
```python
import functools
import math

import jax
import jax.numpy as jnp
from jax import lax
from jax.experimental import pallas as pl
from jax.experimental.pallas import tpu as pltpu
from jax.sharding import PartitionSpec as P

HD = 128
CH = 32
NZ = 16
GZ = 4
STEPS = NZ // GZ
GROUPS = ((0, 4), (4, 4), (8, 4), (12, 2), (14, 2))
KSTEPS = len(GROUPS)
MASKED = -1e30
SCALE = math.log2(math.e) / math.sqrt(HD)
MESH = pl.DeviceIdType.MESH
F32 = jnp.float32
BF16 = jnp.bfloat16


def kernel(
    q_ref, k_ref, v_ref, mask_ref, order_ref, out_ref,
    mask, frames, qbuf, kv, acc, top, osend, lsend, orecv, lrecv, oown, lown, zsend,
    q_sent, k_sent, v_sent, q_got, kv_got, y_sent, y_got,
    x_sent, x_got, other_got, o_sent, l_sent, o_got, l_got, r_sent, r_got, in_got,
):
    b, u = lax.axis_index("blk"), lax.axis_index("uly")
    z, xh = b // 2, b % 2
    y, xl, c = u // 4, (u // 2) % 2, u % 2
    x = xh * 2 + xl
    kpos, qpos = x * (1 - c) + y * c, y * (1 - c) + x * c

    def dev(z2=z, x2=x, y2=y, c2=c):
        return {"blk": z2 * 2 + x2 // 2, "uly": y2 * 4 + (x2 % 2) * 2 + c2}

    def on_key_axis(core, d, c2):
        x2, y2 = lax.rem(x + d * (1 - core), 4), lax.rem(y + d * core, 4)
        return dev(x2=x2, y2=y2, c2=c2)

    def remote(src, dst, send, recv, device):
        return pltpu.make_async_remote_copy(
            src_ref=src, dst_ref=dst, send_sem=send, recv_sem=recv,
            device_id=device, device_id_type=MESH,
        )

    def wait_bytes(ref, sem):
        pltpu.make_async_copy(ref, ref, sem).wait()

    def offset(t):
        return (2 * (t % 2) - 1) * ((t + 1) // 2)

    def source(t):
        return lax.rem(z + NZ + offset(t), NZ)

    def target(t):
        return lax.rem(z + NZ - offset(t), NZ)

    barrier = pltpu.get_barrier_semaphore()
    partners = [dev(z2=target(i)) for i in range(NZ - 1, 0, -1)]
    partners += [dev(y2=lax.rem(y + dy, 4)) for dy in (2, 1, 3)]
    partners += [dev(x2=lax.rem(x + dx, 4)) for dx in (2, 1, 3)]
    partners += [dev(y2=lax.rem(y + dy, 4), c2=1 - c) for dy in (2, 1, 3)]
    partners += [dev(x2=lax.rem(x + dx, 4), c2=1 - c) for dx in (2, 1, 3, 0)]
    for partner in partners:
        pl.semaphore_signal(barrier, inc=1, device_id=partner, device_id_type=MESH)
    mask_copy = pltpu.make_async_copy(mask_ref, mask, in_got.at[0])
    frames_copy = pltpu.make_async_copy(order_ref, frames, in_got.at[1])
    mask_copy.start()
    frames_copy.start()
    pl.semaphore_wait(barrier, len(partners))

    def cols(ref, h):
        return ref.at[:, pl.ds(pl.multiple_of(h * HD, HD), HD)]

    def q_dst(t):
        return qbuf.at[qpos, t, :, pl.ds(0, HD)]

    def kv_dst(t, which):
        return kv.at[t, kpos, which, c, :, pl.ds(0, HD)]

    pltpu.make_async_copy(cols(q_ref, z), q_dst(0), q_got.at[0]).start()
    pltpu.make_async_copy(cols(k_ref, z), kv_dst(0, 0), kv_got.at[0]).start()
    pltpu.make_async_copy(cols(v_ref, z), kv_dst(0, 1), kv_got.at[0]).start()

    def q_copy(t):
        h = target(t)
        return remote(cols(q_ref, h), q_dst(t), q_sent.at[t], q_got.at[t // GZ], dev(z2=h))

    def k_copy(t):
        h = target(t)
        return remote(cols(k_ref, h), kv_dst(t, 0), k_sent.at[t], kv_got.at[t // 4 + t // 14], dev(z2=h))

    def v_copy(t):
        h = target(t)
        return remote(cols(v_ref, h), kv_dst(t, 1), v_sent.at[t], kv_got.at[t // 4 + t // 14], dev(z2=h))

    def start_q(t, carry):
        q_copy(t).start()
        return carry

    def start_kv(t, carry):
        k_copy(t).start()
        v_copy(t).start()
        return carry

    def sent_q(t, carry):
        q_copy(t).wait_send()
        return carry

    def sent_kv(t, carry):
        k_copy(t).wait_send()
        v_copy(t).wait_send()
        return carry

    lax.fori_loop(1, NZ, lambda i, carry: start_q(NZ - i, carry), 0)
    lax.fori_loop(1, NZ, start_kv, 0)

    lane = lax.broadcasted_iota(jnp.int32, (2 * CH, HD), 1)
    mask_copy.wait()
    frames_copy.wait()

    def fill(i, carry):
        t, a = i // 4, i % 4
        first = 2 * source(t)
        key_frame = frames[first + (a // 2) * (1 - c) + xh * c]
        key_tile = y * (1 - c) + a * c
        hot = jnp.where(lane == key_tile * 2 * NZ + key_frame, 1.0, 0.0).astype(BF16)
        kv[t, a, 0, :, :, HD:] = hot.reshape(2, CH, HD)
        kv[t, a, 1, :, :, HD:] = jnp.ones((2, CH, HD), BF16)
        query_frame = frames[first + xh * (1 - c) + (a // 2) * c]
        query_tile = a * (1 - c) + y * c
        rows = jnp.where(mask[query_frame, query_tile] > 0, 0.0, MASKED)
        row = jnp.concatenate([rows[kt : kt + 1] for kt in range(4)], axis=1)
        qbuf[a, t, :, HD:] = jnp.broadcast_to(row, (CH, HD)).astype(BF16)
        return carry

    lax.fori_loop(0, 4 * NZ, fill, 0)

    def zero(i, carry):
        qt, s = i // NZ, i % NZ
        acc[qt, s] = jnp.zeros((CH, 2 * HD), F32)
        top[qt, s] = jnp.full((CH, HD), -3e38, F32)
        return carry

    lax.fori_loop(0, 4 * NZ, zero, 0)

    def q_part(n):
        return qbuf.at[qpos, pl.ds(n * GZ, GZ), :, pl.ds(0, HD)]

    def y_copy(n, dy):
        there = on_key_axis(1 - c, dy, c)
        return remote(q_part(n), q_part(n), y_sent.at[n, dy], y_got.at[n, dy], there)

    for n in range(STEPS):
        wait_bytes(q_part(n), q_got.at[n])
        for dy in (2, 1, 3):
            y_copy(n, dy).start()

    def slots(n):
        return pl.ds(*GROUPS[n])

    def part(n, a):
        return kv.at[slots(n), a, :, c, :, pl.ds(0, HD)]

    def across(n):
        own, there = part(n, kpos), part(n, qpos)
        copies = []
        for d in (2, 1, 3):
            device = on_key_axis(c, d, c)
            copies.append(remote(own, own, x_sent.at[n, d], x_got.at[n, d], device))
            device = on_key_axis(1 - c, d, 1 - c)
            copies.append(remote(own, there, x_sent.at[n, 4 + d], other_got.at[n], device))
        copies.append(remote(own, there, x_sent.at[n, 4], other_got.at[n], dev(c2=1 - c)))
        return copies

    def stage1(n):
        wait_bytes(part(n, kpos), kv_got.at[n])
        for copy in across(n):
            copy.start()

    def stage2(n):
        for d in (1, 3, 2):
            wait_bytes(part(n, lax.rem(kpos + 4 - d, 4)), x_got.at[n, d])
        wait_bytes(kv.at[slots(n), :, :, 1 - c, :, pl.ds(0, HD)], other_got.at[n])

    HB = NZ // 2
    ROWS = HB * CH

    def attend(n, qt, j):
        rows = pl.ds(j * HB, HB)
        qq = qbuf[qt, rows].reshape(ROWS, 2 * HD)
        kk = kv[slots(n), :, 0].reshape(GROUPS[n][1] * 8 * CH, 2 * HD)
        vv = kv[slots(n), :, 1].reshape(GROUPS[n][1] * 8 * CH, 2 * HD)
        s = lax.dot_general(qq, kk, (((1,), (1,)), ((), ())), preferred_element_type=F32)
        old = top[qt, rows].reshape(ROWS, HD)
        new = jnp.maximum(old, jnp.max(s, axis=1, keepdims=True))
        p = jnp.exp2((s - new[:, :1]) * SCALE).astype(BF16)
        pv = jnp.dot(p, vv, preferred_element_type=F32)
        fade = jnp.exp2((old - new) * SCALE)
        total = acc[qt, rows].reshape(ROWS, 2 * HD)
        total = jnp.concatenate([total[:, :HD] * fade, total[:, HD:] * fade], axis=1) + pv
        return total, new

    def attend_store(n, qt, j):
        total, new = attend(n, qt, j)
        acc[qt, pl.ds(j * HB, HB)] = total.reshape(HB, CH, 2 * HD)
        top[qt, pl.ds(j * HB, HB)] = new.reshape(HB, CH, HD)

    stage1(0)
    stage1(1)
    for n in range(STEPS):
        for dy in (2, 1, 3):
            y_copy(n, dy).wait_recv()
    stage2(0)

    def half(n, j):
        for qt in range(4):
            attend_store(n, qt, j)

    half(0, 0)
    stage2(1)
    half(0, 1)
    stage1(2)
    half(1, 0)
    stage1(3)
    half(1, 1)
    stage2(2)
    stage1(4)
    half(2, 0)
    stage2(3)
    half(2, 1)
    half(3, 0)
    half(3, 1)
    stage2(4)

    eye = (
        lax.broadcasted_iota(jnp.int32, (HD, HD), 0) == lax.broadcasted_iota(jnp.int32, (HD, HD), 1)
    )

    def o_copy(d, j):
        return remote(
            osend.at[d, j], orecv.at[d, j], o_sent.at[d, j], o_got.at[d, j],
            on_key_axis(1 - c, d + 1, c),
        )

    def l_copy(d, j):
        return remote(
            lsend.at[d, j], lrecv.at[d, j], l_sent.at[d, j], l_got.at[d, j],
            on_key_axis(1 - c, d + 1, c),
        )

    def last(j, carry):
        for d in (1, 0, 2, 3):
            total, new = attend(KSTEPS - 1, lax.rem(qpos + d + 1, 4), j)
            summed = total[:, HD:]
            o = total[:, :HD] / summed
            lse = new * SCALE + jnp.log2(summed)
            if d == 3:
                oown[j] = o
                lown[j] = lse
            else:
                osend[d, j] = o.astype(BF16).reshape(HB, CH, HD)
                lsend[d, j] = jnp.sum(
                    jnp.where(eye[None], lse.reshape(ROWS // HD, HD, HD), 0.0), axis=1
                )
                o_copy(d, j).start()
                l_copy(d, j).start()
        return carry

    lax.fori_loop(0, 2, lambda i, carry: last(1 - i, carry), 0)

    r_dst = cols(out_ref, z)

    def r_copy(j, i):
        z2 = source(j * HB + i)
        return remote(zsend.at[j, i], r_dst, r_sent.at[j, i], r_got, dev(z2=z2))

    def combine(j, carry):
        parts = [oown[j]]
        weights = [lown[j]]
        for d in range(3):
            o_copy(d, j).wait_recv()
            l_copy(d, j).wait_recv()
            stat = lrecv[d, j]
            wide = jnp.sum(
                jnp.where(eye[None], jnp.broadcast_to(stat[:, None, :], (ROWS // HD, HD, HD)), 0.0),
                axis=2, keepdims=True,
            )
            weights.append(jnp.broadcast_to(wide, (ROWS // HD, HD, HD)).reshape(ROWS, HD))
            parts.append(orecv[d, j].reshape(ROWS, HD).astype(F32))
        high = functools.reduce(jnp.maximum, weights)
        weights = [jnp.exp2(w - high) for w in weights]
        mixed = sum(w * o for w, o in zip(weights, parts)) / sum(weights)
        zsend[j] = mixed.astype(BF16).reshape(HB, CH, HD)

        def home(i, carry2):
            r_copy(j, i).start()
            return carry2

        lax.fori_loop(1 - j, HB, home, 0)
        return carry

    combine(1, 0)
    combine(0, 0)
    pltpu.make_async_copy(zsend.at[0, 0], r_dst, r_got).start()
    wait_bytes(out_ref, r_got)

    lax.fori_loop(1, NZ, sent_q, 0)
    lax.fori_loop(1, NZ, sent_kv, 0)
    def drain_y(n, carry):
        for dy in (2, 1, 3):
            y_copy(n, dy).wait_send()
        return carry

    lax.fori_loop(0, STEPS, drain_y, 0)

    for n in range(KSTEPS):
        for copy in across(n):
            copy.wait_send()

    def drain_o(j, carry):
        for d in range(3):
            o_copy(d, j).wait_send()
            l_copy(d, j).wait_send()
        return carry

    lax.fori_loop(0, 2, drain_o, 0)

    def drain_r(i, carry):
        r_copy(i // HB, i % HB).wait_send()
        return carry

    lax.fori_loop(1, NZ, drain_r, 0)


def attention(queries, keys, values, tile_mask, frame_order):
    dma = pltpu.SemaphoreType.DMA
    hbm = pl.BlockSpec(memory_space=pl.ANY)
    return pl.pallas_call(
        kernel,
        out_shape=jax.ShapeDtypeStruct(queries.shape, BF16),
        in_specs=[hbm] * 5,
        out_specs=hbm,
        scratch_shapes=[
            pltpu.VMEM((2 * NZ, 4, 4, 2 * NZ), jnp.int32),
            pltpu.SMEM((2 * NZ,), jnp.int32),
            pltpu.VMEM((4, NZ, CH, 2 * HD), BF16),
            pltpu.VMEM((NZ, 4, 2, 2, CH, 2 * HD), BF16),
            pltpu.VMEM((4, NZ, CH, 2 * HD), F32),
            pltpu.VMEM((4, NZ, CH, HD), F32),
            pltpu.VMEM((3, 2, NZ // 2, CH, HD), BF16),
            pltpu.VMEM((3, 2, 2, HD), F32),
            pltpu.VMEM((3, 2, NZ // 2, CH, HD), BF16),
            pltpu.VMEM((3, 2, 2, HD), F32),
            pltpu.VMEM((2, NZ // 2 * CH, HD), F32),
            pltpu.VMEM((2, NZ // 2 * CH, HD), F32),
            pltpu.VMEM((2, NZ // 2, CH, HD), BF16),
            dma((NZ,)), dma((NZ,)), dma((NZ,)),
            dma((STEPS,)), dma((KSTEPS,)),
            dma((STEPS, 4)), dma((STEPS, 4)),
            dma((KSTEPS, 8)), dma((KSTEPS, 4)), dma((KSTEPS,)),
            dma((3, 2)), dma((3, 2)), dma((3, 2)), dma((3, 2)),
            dma((2, NZ // 2)), dma, dma((2,)),
        ],
        compiler_params=pltpu.CompilerParams(
            collective_id=0, has_side_effects=True, vmem_limit_bytes=56 * 2**20
        ),
        name="attention",
    )(queries, keys, values, tile_mask, frame_order)


def per_device(queries, keys, values, tile_mask, frame_order):
    by_key = jnp.transpose(tile_mask, (0, 2, 3, 1))
    return attention(queries, keys, values, by_key, frame_order)


def solution(mesh):
    rows = P(("blk", "uly"), None)
    return jax.shard_map(
        per_device,
        mesh=mesh,
        in_specs=(rows, rows, rows, P(), P()),
        out_specs=rows,
        check_vma=False,
    )
```

time: 80.9 us -> 68.9 us (0.85); the launches traced: 79.8 us -> 68.8 us
  Pallas kernels: 78.2 us -> 67.2 us
    pallas_call x1, Pallas kernels: 78.2 us -> 67.2 us  [attention(): pl.pallas_call(kernel, out_shape=jax.ShapeDtypeStruct(queries.shape, BF16...]
where the time goes in v3:
time: 68.9 us; the launch traced here: 68.8 us
  Pallas kernels  67.2 us (98%)
  local copies, waits for them, and re-layouts  1.57 us (2%)
    pallas_call x1, Pallas kernels, attention(): pl.pallas_call(kernel, out_shape=jax.ShapeDtypeStruct(queries.shape, BF16...  67.2 us
    unnamed x1, local copies, waits for them, and re-layouts  1.57 us

profile of v3, /device:TPU:1, one launch (start us, length us, event | category | flops | bytes accessed | tf_op | source)
XLA Modules:
  0.0 68.8 jit_solution(14921622828058244679)
XLA Ops:
  0.0 67.2 %attention.1 = bf16[32,2048]{1,0:T(8,128)(2,1)} custom-call(bf16[32,2048]{1,0:T(8,128)(2,1)} %q_ref.1, bf16[32,2048]{1,0:T(8,128)(2,1)} %k_ref.1, bf16[32,2048]{1,0:T(8,128)(2,1)} %v_ref.1, s32[32,4,4,32]{3,2,1,0:T(4,128)} %bitcast.1, s32[32]{0:T(128)} %order_ref.1), custom_call_target="tpu_custom_call" | custom-call | tf_op jit(solution)/shard_map/attention/pallas_call | solution.py:343
  67.2 1.6 %copy.7 = bf16[32,2048]{1,0:T(8,128)(2,1)} copy(bf16[32,2048]{1,0:T(8,128)(2,1)} %attention.1) | data formatting | bytes 262144

commit v4 on v3

--- a/solution.py
+++ b/solution.py
@@ -13,7 +13,7 @@
 NZ = 16
 GZ = 4
 STEPS = NZ // GZ
-GROUPS = ((0, 4), (4, 4), (8, 4), (12, 2), (14, 2))
+GROUPS = ((0, 2), (2, 4), (6, 4), (10, 2), (12, 2), (14, 2))
 KSTEPS = len(GROUPS)
 MASKED = -1e30
 SCALE = math.log2(math.e) / math.sqrt(HD)
@@ -92,11 +92,11 @@
 
     def k_copy(t):
         h = target(t)
-        return remote(cols(k_ref, h), kv_dst(t, 0), k_sent.at[t], kv_got.at[t // 4 + t // 14], dev(z2=h))
+        return remote(cols(k_ref, h), kv_dst(t, 0), k_sent.at[t], kv_got.at[(t + 2) // 4 + t // 12], dev(z2=h))
 
     def v_copy(t):
         h = target(t)
-        return remote(cols(v_ref, h), kv_dst(t, 1), v_sent.at[t], kv_got.at[t // 4 + t // 14], dev(z2=h))
+        return remote(cols(v_ref, h), kv_dst(t, 1), v_sent.at[t], kv_got.at[(t + 2) // 4 + t // 12], dev(z2=h))
 
     def start_q(t, carry):
         q_copy(t).start()
@@ -221,21 +221,32 @@
         for qt in range(4):
             attend_store(n, qt, j)
 
+    def both(n):
+        def one(j, carry):
+            half(n, j)
+            return carry
+
+        lax.fori_loop(0, 2, one, 0)
+
     half(0, 0)
-    stage2(1)
     half(0, 1)
     stage1(2)
+    stage2(1)
     half(1, 0)
+    half(1, 1)
     stage1(3)
-    half(1, 1)
     stage2(2)
     stage1(4)
     half(2, 0)
+    half(2, 1)
     stage2(3)
-    half(2, 1)
+    stage1(5)
     half(3, 0)
     half(3, 1)
     stage2(4)
+    half(4, 0)
+    half(4, 1)
+    stage2(5)
 
     eye = (
         lax.broadcasted_iota(jnp.int32, (HD, HD), 0) == lax.broadcasted_iota(jnp.int32, (HD, HD), 1)
@@ -298,10 +309,10 @@
         zsend[j] = mixed.astype(BF16).reshape(HB, CH, HD)
 
         def home(i, carry2):
-            r_copy(j, i).start()
+            r_copy(j, HB - 1 - i).start()
             return carry2
 
-        lax.fori_loop(1 - j, HB, home, 0)
+        lax.fori_loop(0, HB - 1 + j, home, 0)
         return carry
 
     combine(1, 0)

time: 68.9 us -> 67.8 us (0.984)
  Pallas kernels: 67.2 us -> 66.1 us
    pallas_call x1, Pallas kernels: 67.2 us -> 66.1 us  [attention(): pl.pallas_call(kernel, out_shape=jax.ShapeDtypeStruct(queries.shape, BF16...]
where the time goes in v4:
time: 67.8 us; the launch traced here: 67.7 us
  Pallas kernels  66.1 us (97%)
  local copies, waits for them, and re-layouts  1.57 us (2%)
    pallas_call x1, Pallas kernels, attention(): pl.pallas_call(kernel, out_shape=jax.ShapeDtypeStruct(queries.shape, BF16...  66.1 us
    unnamed x1, local copies, waits for them, and re-layouts  1.57 us

profile of v4, /device:TPU:1, one launch (start us, length us, event | category | flops | bytes accessed | tf_op | source)
XLA Modules:
  0.0 67.7 jit_solution(1709262943780328173)
XLA Ops:
  0.0 66.1 %attention.1 = bf16[32,2048]{1,0:T(8,128)(2,1)} custom-call(bf16[32,2048]{1,0:T(8,128)(2,1)} %q_ref.1, bf16[32,2048]{1,0:T(8,128)(2,1)} %k_ref.1, bf16[32,2048]{1,0:T(8,128)(2,1)} %v_ref.1, s32[32,4,4,32]{3,2,1,0:T(4,128)} %bitcast.1, s32[32]{0:T(128)} %order_ref.1), custom_call_target="tpu_custom_call" | custom-call | tf_op jit(solution)/shard_map/attention/pallas_call | solution.py:354
  66.1 1.6 %copy.7 = bf16[32,2048]{1,0:T(8,128)(2,1)} copy(bf16[32,2048]{1,0:T(8,128)(2,1)} %attention.1) | data formatting | bytes 262144
